TPU v7x, 512 devices: a whole 4x8x8 slice. The times are simulated.
512 devices in a mesh: frames: 64 (over z, x, core), pix: 8 (over y).
Axes of the slice: x: 4, y: 8, z: 8, core: 2. Of those that a mesh axis runs over, the one named last changes fastest.
Arguments:
- counts: int32 [4096, 65536], P('frames', 'pix'), may hold values from 0 to 64
- weights: float32 [16, 4096], P(None, 'frames'), may hold values from 0.025 to 3, as said below
- maps: float32 [16, 65536], P(None, 'pix'), may hold values from 0.1 to 1
Outputs:
- new_weights: float32 [16, 4096], P(None, 'frames')
- new_maps: float32 [16, 65536], P(None, 'pix')
Inputs may be any that keep to these rules, and one draw needn't show every extreme that they name: `weights`: positive.
All inputs are finite; a program needn't handle non-finite values.
Results may differ from a plain program's by a relative error of at most 0.0001.
Values sent between devices are 32-bit elements; how exact they have to be, the bound alone decides.
A program may use at most 64 MiB of HBM per device.

v0:
```python
import jax
import jax.numpy as jnp
from jax import lax
from jax.sharding import PartitionSpec as P

ITERS = 2


def local(counts, weights, maps):
    high = lax.Precision.HIGHEST
    observed = counts.astype(jnp.float32)
    wmat = weights
    hmat = maps
    for step in range(ITERS):
        model = jnp.dot(wmat.T, hmat, precision=high)
        numer_part = jnp.dot(wmat, observed / model, precision=high)
        wsum_part = jnp.sum(wmat, axis=1)
        numer, wsum = lax.psum((numer_part, wsum_part), "frames")
        hmat = hmat * numer / wsum[:, None]
        model = jnp.dot(wmat.T, hmat, precision=high)
        ratio = observed / model
        wnum_part = lax.dot_general(hmat, ratio, (((1,), (1,)), ((), ())), precision=high)
        hsum_part = jnp.sum(hmat, axis=1)
        wnum, hsum = lax.psum((wnum_part, hsum_part), "pix")
        wmat = wmat * wnum / hsum[:, None]
    return (wmat, hmat)


def solution(mesh):
    placed = (P("frames", "pix"), P(None, "frames"), P(None, "pix"))
    return jax.shard_map(
        local,
        mesh=mesh,
        in_specs=placed,
        out_specs=(P(None, "frames"), P(None, "pix")),
        check_vma=False,
    )
```

profile of v0, /device:TPU:1, one launch (start us, length us, event | category | flops | bytes accessed | tf_op | source)
XLA Modules:
  0.0 452.2 jit_solution(11719860500418482116)
XLA Ops:
  7.2 0.0 all-reduce.5.cloned.1.call-start
  7.2 3.7 convolution_divide_fusion.2
  11.0 0.0 copy-start.3
  11.0 2.0 convolution_bitcast_fusion.1
  13.0 0.0 all-reduce.5.cloned.1.call-update
  13.0 0.0 all-reduce.7.cloned.1.call-start
  13.0 0.1 reduce_sum.36
  13.2 131.2 %psum.57 = f32[16]{0:T(128)S(1)} all-reduce(f32[16]{0:T(128)S(1)} %reduce_sum.36), channel_id=1, replica_groups=mesh['frames'=64,'pix'=8] {'frames'}, use_global_device_ids=true, to_apply=%region_2.0 | all-reduce | flops 16 | bytes 128 | tf_op jit(solution)/shard_map/psum | solution.py:18
  144.4 66.3 %all-reduce.5.cloned.1.call-done = f32[16,8192]{1,0:T(8,128)} async-done(((f32[16,8192]{1,0:T(8,128)}), f32[16,8192]{1,0:T(8,128)}) %all-reduce.5.cloned.1.call-update) | async-done | bytes 524304 | tf_op jit(solution)/shard_map/psum | solution.py:18
  210.7 1.3 fusion.3
  212.1 2.0 fusion
  214.0 1.7 fusion.4
  215.8 13.7 %all-reduce.1 = (f32[16,64]{1,0:T(8,128)S(1)}, f32[16]{0:T(128)S(1)}) all-reduce(f32[16,64]{1,0:T(8,128)S(1)} %fusion.4, f32[16]{0:T(128)S(1)} %get-tuple-element.10), channel_id=1, replica_groups=mesh['frames'=64,'pix'=8] {'pix'}, use_global_device_ids=true, to_apply=%region_3.0 | all-reduce | flops 1040 | bytes 8320 | tf_op jit(solution)/shard_map/psum | solution.py:24
  229.5 0.2 fusion.2
  229.7 2.0 convolution_divide_fusion.1
  231.6 1.9 fusion.5
  233.5 0.0 all-reduce.7.cloned.1.call-update
  233.6 130.1 %psum.61 = f32[16]{0:T(128)S(1)} all-reduce(f32[16]{0:T(128)S(1)} %get-tuple-element.8), channel_id=1, replica_groups=mesh['frames'=64,'pix'=8] {'frames'}, use_global_device_ids=true, to_apply=%region_8.0 | all-reduce | flops 16 | bytes 128 | tf_op jit(solution)/shard_map/psum | solution.py:18
  363.7 62.2 %all-reduce.7.cloned.1.call-done = f32[16,8192]{1,0:T(8,128)} async-done(((f32[16,8192]{1,0:T(8,128)}), f32[16,8192]{1,0:T(8,128)}) %all-reduce.7.cloned.1.call-update) | async-done | bytes 524304 | tf_op jit(solution)/shard_map/psum | solution.py:18
  425.9 1.3 fusion.1
  427.2 2.0 convolution_divide_fusion
  429.2 1.7 fusion.6
  431.0 13.7 %all-reduce = (f32[16,64]{1,0:T(8,128)S(1)}, f32[16]{0:T(128)S(1)}) all-reduce(f32[16,64]{1,0:T(8,128)S(1)} %fusion.6, f32[16]{0:T(128)S(1)} %get-tuple-element.6), channel_id=1, replica_groups=mesh['frames'=64,'pix'=8] {'pix'}, use_global_device_ids=true, to_apply=%region_9.0 | all-reduce | flops 1040 | bytes 8320 | tf_op jit(solution)/shard_map/psum | solution.py:24
  444.7 0.7 multiply_divide_fusion.2
  (7 shorter events, 0.0 us)
Async XLA Ops:
  7.2 3.8 copy-start.2
  7.2 203.6 %all-reduce.5.cloned.1.call-start = ((), (), s32[]{:S(2)}) async-start(), calls=%async_computation | async-start | bytes 1048576 | tf_op jit(solution)/shard_map/psum | solution.py:18
  11.0 199.8 %copy-start.1 = (f32[16,8192]{1,0:T(8,128)S(1)}, f32[16,8192]{1,0:T(8,128)}, u32[]{:S(2)}) copy-start(f32[16,8192]{1,0:T(8,128)} %param.5) | copy-start | bytes 1572868
  11.0 201.1 %copy-start.3 = (s32[64,8192]{1,0:T(8,128)S(1)}, s32[64,8192]{1,0:T(8,128)}, u32[]{:S(2)}) copy-start(s32[64,8192]{1,0:T(8,128)} %param.3) | copy-start | bytes 6291460
  13.0 412.9 %all-reduce.7.cloned.1.call-start = ((), (), s32[]{:S(2)}) async-start(), calls=%async_computation.1 | async-start | bytes 1048576 | tf_op jit(solution)/shard_map/psum | solution.py:18
  427.2 2.0 copy-start
Sparse Core Ops, SparseCore 0:
  13.1 197.5 all-reduce.4
  233.7 192.1 all-reduce.6
where the time goes:
time: 457 us; the launch traced here: 452 us
  blocking collectives  289 us (63%)
  waiting for transfers between devices  129 us (28%)
  matrix products  17 us (4%)
  between operations  14.1 us (3%)
    psum x2, blocking collectives, local(): numer, wsum = lax.psum((numer_part, wsum_part), 'frames')  261 us
    psum x2, waiting for transfers between devices, local(): numer, wsum = lax.psum((numer_part, wsum_part), 'frames')  129 us
    psum x2, blocking collectives, local(): wnum, hsum = lax.psum((wnum_part, hsum_part), 'pix')  27.4 us
    dot_general x4, matrix products, local(): model = jnp.dot(wmat.T, hmat, precision=high)  9.64 us
  transfers between devices with their start and end apart: 2, of which 2 were waited for; matrix products, arithmetic and copies ran while one was open for 0% of the time, Pallas kernels for 0%

commit v1 on v0

v1 whole, which is shorter than its diff:
```python
import functools

import jax
import jax.numpy as jnp
from jax import lax
from jax.experimental import pallas as pl
from jax.experimental.pallas import tpu as pltpu
from jax.sharding import PartitionSpec as P

MESH = pl.DeviceIdType.MESH
F32 = jnp.float32
BF16 = jnp.bfloat16
ITERS = 2
NZ, NX, NY = 8, 4, 8
K = 16
LANES = 128
FRAMES = 64
HALF = NZ * NX
PIECE = 16
PIX = 2 * HALF * LANES


def hops(offset):
    dz, dx = offset
    return min(dz, NZ - dz) + min(dx, NX - dx)


OFFSETS = sorted(((dz, dx) for dz in range(NZ) for dx in range(NX) if dz or dx), key=lambda o: -hops(o))
SLOT = {offset: i for i, offset in enumerate(OFFSETS)}
Y_OFFSETS = (4, 3, 5, 2, 6, 1, 7)


def split(x):
    hi = x.astype(BF16)
    return hi, (x - hi.astype(F32)).astype(BF16)


def weight_operands(w):
    hi, lo = split(w)
    for_model = jnp.concatenate([hi, hi, lo, lo], axis=0)
    for_maps = jnp.concatenate([jnp.concatenate([hi, hi], axis=1), jnp.concatenate([lo, lo], axis=1)], axis=0)
    return for_model, for_maps


def load_maps(h_ref, first, count):
    return jnp.concatenate([h_ref[first + i] for i in range(count)], axis=1)


def ratios(c_ref, h, for_model, first, count):
    hi, lo = split(h)
    model = lax.dot_general(
        for_model,
        jnp.concatenate([hi, lo, hi, lo], axis=0),
        (((0,), (0,)), ((), ())),
        preferred_element_type=F32,
    )
    width = count * LANES
    counts = c_ref[:, pl.ds(pl.multiple_of(first * LANES, width), width)].astype(F32)
    r_hi, r_lo = split(counts / model)
    return jnp.concatenate([r_hi, r_lo], axis=0), jnp.concatenate([hi, lo], axis=0)


def to_row(column):
    shape = (K, LANES)
    diagonal = lax.broadcasted_iota(jnp.int32, shape, 0) == lax.broadcasted_iota(jnp.int32, shape, 1)
    return jnp.sum(jnp.where(diagonal, column, 0.0), axis=0, keepdims=True)


def to_column(row):
    shape = (K, LANES)
    diagonal = lax.broadcasted_iota(jnp.int32, shape, 0) == lax.broadcasted_iota(jnp.int32, shape, 1)
    return jnp.sum(jnp.where(diagonal, row, 0.0), axis=1, keepdims=True)


def kernel(
    c_hbm, w_ref, h_hbm, w_out, h_out,
    c_ref, h_in, h_ref, numer, from_core, partial, parts, chunk_sum, row_src, row_core, row_sum, rows, y_src, y_parts,
    load_sem, core_send, core_recv, part_send, part_recv, map_send, map_recv, half_send, half_recv,
    rowc_send, rowc_recv, row_send, row_recv, y_send, y_recv,
):
    f = lax.axis_index("frames")
    y = lax.axis_index("pix")
    z, x, core = f // (2 * NX), lax.rem(f // 2, NX), lax.rem(f, 2)

    def device(dz, dx):
        zz, xx = lax.rem(z + dz, NZ), lax.rem(x + dx, NX)
        return zz * NX + xx, ((zz * NX + xx) * 2 + core, y)

    sibling = (f + 1 - 2 * core, y)
    y_devices = [(f, lax.rem(y + d, NY)) for d in Y_OFFSETS]

    own_half = pl.multiple_of(core * HALF, HALF)
    other_half = pl.multiple_of((1 - core) * HALF, HALF)
    own = z * NX + x

    barrier = pltpu.get_barrier_semaphore()
    for offset in OFFSETS:
        pl.semaphore_signal(barrier, inc=1, device_id=device(*offset)[1], device_id_type=MESH)
    for d in [sibling] + y_devices:
        pl.semaphore_signal(barrier, inc=1, device_id=d, device_id_type=MESH)

    loads = []
    for i, first in enumerate((other_half, own_half)):
        columns = pl.ds(pl.multiple_of(first * LANES, HALF * LANES), HALF * LANES)
        loads.append(pltpu.make_async_copy(h_hbm.at[:, columns], h_in.at[:, columns], load_sem.at[2 * i]))
        loads.append(pltpu.make_async_copy(c_hbm.at[:, columns], c_ref.at[:, columns], load_sem.at[2 * i + 1]))
    for load in loads:
        load.start()

    def unpack(first):
        for i in range(HALF):
            column = pl.multiple_of((first + i) * LANES, LANES)
            h_ref[0, first + i] = h_in[:, pl.ds(column, LANES)]

    def remote(src, dst, send, recv, to):
        return pltpu.make_async_remote_copy(
            src_ref=src, dst_ref=dst, send_sem=send, recv_sem=recv, device_id=to, device_id_type=MESH
        )

    w = w_ref[...]
    for it in range(ITERS):
        h_now, h_next = h_ref.at[it], h_ref.at[it + 1]
        for_model, for_maps = weight_operands(w)
        w_total = jnp.sum(w, axis=1, keepdims=True)
        row_src[it] = to_row(w_total)

        def numerators(first, at, out):
            rc, _ = ratios(c_ref, load_maps(h_now, first + at, PIECE), for_model, first + at, PIECE)
            both = jnp.dot(for_maps, rc, preferred_element_type=F32)
            both = both[:K] + both[K:]
            for i in range(PIECE):
                out[at + i] = both[:, i * LANES : (i + 1) * LANES]

        if it == 0:
            loads[0].wait()
            loads[1].wait()
            unpack(other_half)
        else:
            row_copy = remote(row_src.at[it], row_core.at[it], rowc_send.at[it], rowc_recv.at[it], sibling)
            row_copy.start()
        core_copies = []
        for piece in range(HALF // PIECE):
            numerators(other_half, piece * PIECE, numer.at[it])
            if it == 0 and piece == 0:
                pl.semaphore_wait(barrier, len(OFFSETS) + 1 + len(y_devices))
                row_copy = remote(row_src.at[it], row_core.at[it], rowc_send.at[it], rowc_recv.at[it], sibling)
                row_copy.start()
            chunks = pl.ds(piece * PIECE, PIECE)
            copy = remote(
                numer.at[it, chunks], from_core.at[it, chunks],
                core_send.at[it, piece], core_recv.at[it, piece], sibling,
            )
            copy.start()
            core_copies.append(copy)
        if it == 0:
            loads[2].wait()
            loads[3].wait()
            unpack(own_half)
        for piece in range(HALF // PIECE):
            numerators(own_half, piece * PIECE, partial.at[it])

        row_copy.wait()
        row_sum[it] = row_src[it] + row_core[it]
        for offset in OFFSETS:
            remote(
                row_sum.at[it], rows.at[it, SLOT[offset]], row_send.at[it], row_recv.at[it], device(*offset)[1]
            ).start()
        for piece, copy in enumerate(core_copies):
            copy.wait()
            chunks = pl.ds(piece * PIECE, PIECE)
            partial[it, chunks] = partial[it, chunks] + from_core[it, chunks]
        for offset in OFFSETS:
            chunk, to = device(*offset)
            remote(
                partial.at[it, chunk], parts.at[it, SLOT[offset]], part_send.at[it], part_recv.at[it], to
            ).start()
        pltpu.make_async_copy(rows.at[it], rows.at[it], row_recv.at[it]).wait()
        pltpu.make_async_copy(rows.at[it], rows.at[it], row_send.at[it]).wait()
        c_total = to_column(row_sum[it] + jnp.sum(rows[it], axis=0))
        pltpu.make_async_copy(parts.at[it], parts.at[it], part_recv.at[it]).wait()
        numer_total = partial[it, own] + jnp.sum(parts[it], axis=0)
        mine = own_half + own
        h_next[mine] = h_now[mine] * numer_total / c_total

        for offset in OFFSETS:
            _, to = device(*offset)
            remote(h_next.at[mine], h_next.at[mine], map_send.at[it], map_recv.at[it], to).start()
        pltpu.make_async_copy(parts.at[it], parts.at[it], part_send.at[it]).wait()
        pltpu.make_async_copy(parts.at[it], parts.at[it], map_recv.at[it]).wait()
        half = h_next.at[pl.ds(own_half, HALF)]
        half_copy = remote(half, half, half_send.at[it], half_recv.at[it], sibling)
        half_copy.start()

        def weight_numerators(first, total, sums):
            for piece in range(HALF // PIECE):
                at = first + piece * PIECE
                h = load_maps(h_next, at, PIECE)
                rc, hc = ratios(c_ref, h, for_model, at, PIECE)
                total += lax.dot_general(hc, rc, (((1,), (1,)), ((), ())), preferred_element_type=F32)
                for i in range(PIECE):
                    sums += h[:, i * LANES : (i + 1) * LANES]
            return total, sums

        total, sums = weight_numerators(own_half, jnp.zeros((2 * K, 2 * FRAMES), F32), jnp.zeros((K, LANES), F32))
        half_copy.wait_recv()
        total, sums = weight_numerators(other_half, total, sums)
        total = total[:K] + total[K:]
        total = total[:, :FRAMES] + total[:, FRAMES:]
        h_total = jnp.sum(sums, axis=1, keepdims=True)
        y_src[it] = jnp.concatenate([total, jnp.broadcast_to(h_total, (K, LANES - FRAMES))], axis=1)
        for i, to in enumerate(y_devices):
            remote(y_src.at[it], y_parts.at[it, i], y_send.at[it], y_recv.at[it], to).start()
        pltpu.make_async_copy(parts.at[it], parts.at[it], map_send.at[it]).wait()
        half_copy.wait_send()
        if it == ITERS - 1:
            for i in range(2 * HALF):
                h_out[:, i * LANES : (i + 1) * LANES] = h_next[i]
        pltpu.make_async_copy(y_parts.at[it], y_parts.at[it], y_recv.at[it]).wait()
        pltpu.make_async_copy(y_parts.at[it], y_parts.at[it], y_send.at[it]).wait()
        total = y_src[it] + jnp.sum(y_parts[it], axis=0)
        w = w * total[:, :FRAMES] / total[:, FRAMES : FRAMES + 1]
    w_out[...] = w


def local(counts, weights, maps):
    n = len(OFFSETS)
    dma = pltpu.SemaphoreType.DMA
    pieces = HALF // PIECE
    return pl.pallas_call(
        kernel,
        out_shape=(jax.ShapeDtypeStruct(weights.shape, F32), jax.ShapeDtypeStruct(maps.shape, F32)),
        in_specs=[
            pl.BlockSpec(memory_space=pl.ANY),
            pl.BlockSpec(memory_space=pltpu.VMEM),
            pl.BlockSpec(memory_space=pl.ANY),
        ],
        out_specs=(pl.BlockSpec(memory_space=pltpu.VMEM), pl.BlockSpec(memory_space=pltpu.VMEM)),
        scratch_shapes=[
            pltpu.VMEM((FRAMES, PIX), jnp.int32),
            pltpu.VMEM((K, PIX), F32),
            pltpu.VMEM((ITERS + 1, 2 * HALF, K, LANES), F32),
            pltpu.VMEM((ITERS, HALF, K, LANES), F32),
            pltpu.VMEM((ITERS, HALF, K, LANES), F32),
            pltpu.VMEM((ITERS, HALF, K, LANES), F32),
            pltpu.VMEM((ITERS, n, K, LANES), F32),
            pltpu.VMEM((K, LANES), F32),
            pltpu.VMEM((ITERS, 1, LANES), F32),
            pltpu.VMEM((ITERS, 1, LANES), F32),
            pltpu.VMEM((ITERS, 1, LANES), F32),
            pltpu.VMEM((ITERS, n, 1, LANES), F32),
            pltpu.VMEM((ITERS, K, LANES), F32),
            pltpu.VMEM((ITERS, NY - 1, K, LANES), F32),
            dma((4,)),
            dma((ITERS, pieces)),
            dma((ITERS, pieces)),
            dma((ITERS,)),
            dma((ITERS,)),
            dma((ITERS,)),
            dma((ITERS,)),
            dma((ITERS,)),
            dma((ITERS,)),
            dma((ITERS,)),
            dma((ITERS,)),
            dma((ITERS,)),
            dma((ITERS,)),
            dma((ITERS,)),
            dma((ITERS,)),
        ],
        compiler_params=pltpu.CompilerParams(
            collective_id=0, has_side_effects=True, vmem_limit_bytes=32 * 1024 * 1024
        ),
        name="nmf_updates",
    )(counts, weights, maps)


def solution(mesh):
    return jax.shard_map(
        local,
        mesh=mesh,
        in_specs=(P("frames", "pix"), P(None, "frames"), P(None, "pix")),
        out_specs=(P(None, "frames"), P(None, "pix")),
        check_vma=False,
    )
```

time: 457 us -> 73.8 us (0.16)
  blocking collectives: 289 us -> 0 us
  waiting for transfers between devices: 129 us -> 0 us
  Pallas kernels: 0 us -> 68.2 us
  matrix products: 17 us -> 0 us
  between operations: 14.1 us -> 0.65 us
  local copies, waits for them, and re-layouts: 0.02 us -> 4.72 us
    psum x4 -> x0, blocking collectives: 289 us -> none  [the longest x2 261 us: local(): numer, wsum = lax.psum((numer_part, wsum_part), 'frames')]
    psum x2 -> x0, waiting for transfers between devices: 129 us -> none  [local(): numer, wsum = lax.psum((numer_part, wsum_part), 'frames')]
    pallas_call x0 -> x1, Pallas kernels: none -> 68.2 us  [local(): pl.pallas_call(kernel, out_shape=(jax.ShapeDtypeStruct(weights.shape, F32...]
    dot_general x8 -> x0, matrix products: 17 us -> none  [the longest x4 9.64 us: local(): model = jnp.dot(wmat.T, hmat, precision=high)]
    unnamed x8, local copies, waits for them, and re-layouts: 0.02 us -> 4.72 us
  transfers between devices with their start and end apart: 2 -> 0, of which waited for: 2 -> 0; matrix products, arithmetic and copies ran while one was open for 0% -> 0% of each run, Pallas kernels for 0% -> 0%
where the time goes in v1:
time: 73.8 us; the launch traced here: 73.5 us
  Pallas kernels  68.2 us (92%)
  local copies, waits for them, and re-layouts  4.72 us (6%)
    pallas_call x1, Pallas kernels, local(): pl.pallas_call(kernel, out_shape=(jax.ShapeDtypeStruct(weights.shape, F32...  68.2 us
    unnamed x8, local copies, waits for them, and re-layouts  4.72 us

profile of v1, /device:TPU:1, one launch (start us, length us, event | category | flops | bytes accessed | tf_op | source)
XLA Modules:
  0.0 73.5 jit_solution(10704528063232668759)
XLA Ops:
  0.6 0.0 copy-start
  0.6 1.6 %copy-done = s32[64,8192]{1,0:T(8,128)S(1)} copy-done((s32[64,8192]{1,0:T(8,128)S(1)}, s32[64,8192]{1,0:T(8,128)}, u32[]{:S(2)}) %copy-start) | copy-done | bytes 2097176
  2.2 0.0 copy-start.1
  2.2 1.0 %copy-done.1 = f32[16,8192]{1,0:T(8,128)S(1)} copy-done((f32[16,8192]{1,0:T(8,128)S(1)}, f32[16,8192]{1,0:T(8,128)}, u32[]{:S(2)}) %copy-start.1) | copy-done | bytes 524312
  3.3 0.0 copy-start.2
  3.3 0.7 copy-done.2
  4.0 68.2 %nmf_updates.1 = (f32[16,64]{1,0:T(8,128)S(1)}, f32[16,8192]{1,0:T(8,128)S(1)}) custom-call(s32[64,8192]{1,0:T(8,128)S(1)} %copy-done, f32[16,64]{1,0:T(8,128)S(1)} %copy-done.2, f32[16,8192]{1,0:T(8,128)S(1)} %copy-done.1), custom_call_target="tpu_custom_call" | custom-call | tf_op jit(solution)/shard_map/nmf_updates/pallas_call | solution.py:229
  72.1 0.6 copy.7
  72.7 0.8 %copy.8 = f32[16,8192]{1,0:T(8,128)} copy(f32[16,8192]{1,0:T(8,128)S(1)} %get-tuple-element.5) | data formatting | bytes 1048576
Async XLA Ops:
  0.6 1.6 %copy-start = (s32[64,8192]{1,0:T(8,128)S(1)}, s32[64,8192]{1,0:T(8,128)}, u32[]{:S(2)}) copy-start(s32[64,8192]{1,0:T(8,128)} %c_hbm.1) | copy-start | bytes 6291460
  2.2 1.0 %copy-start.1 = (f32[16,8192]{1,0:T(8,128)S(1)}, f32[16,8192]{1,0:T(8,128)}, u32[]{:S(2)}) copy-start(f32[16,8192]{1,0:T(8,128)} %h_hbm.1) | copy-start | bytes 1572868
  3.3 0.7 copy-start.2

commit v2 on v1

v2 whole, which is shorter than its diff:
```python
import functools

import jax
import jax.numpy as jnp
from jax import lax
from jax.experimental import pallas as pl
from jax.experimental.pallas import tpu as pltpu
from jax.sharding import PartitionSpec as P

MESH = pl.DeviceIdType.MESH
F32 = jnp.float32
BF16 = jnp.bfloat16
ITERS = 2
NZ, NX, NY = 8, 4, 8
K = 16
LANES = 128
FRAMES = 64
HALF = NZ * NX
PIX = 2 * HALF * LANES


def hops(offset):
    dz, dx = offset
    return min(dz, NZ - dz) + min(dx, NX - dx)


OFFSETS = sorted(((dz, dx) for dz in range(NZ) for dx in range(NX) if dz or dx), key=lambda o: (-min(o[1], NX - o[1]), -min(o[0], NZ - o[0])))
SLOT = {offset: i for i, offset in enumerate(OFFSETS)}
Y_OFFSETS = (4, 3, 5, 2, 6, 1, 7)
FAR_FIRST = (4, 3, 5, 2, 6, 1, 7, 0)
NEAR_FIRST = (0, 1, 7, 2, 6, 3, 5, 4)
GROUPS = 4
PIECES = NZ // GROUPS
GROUP_PIX = NX * LANES
PIECE = GROUPS * NX
PARTS = 2
ROWS = K // PARTS


def split(x):
    hi = x.astype(BF16)
    return hi, (x - hi.astype(F32)).astype(BF16)


def weight_operands(w):
    hi, lo = split(w)
    for_model = jnp.concatenate([hi, hi, lo, lo], axis=0)
    for_maps = jnp.concatenate([jnp.concatenate([hi, hi], axis=1), jnp.concatenate([lo, lo], axis=1)], axis=0)
    return for_model, for_maps


def columns(chunk, count):
    return pl.ds(pl.multiple_of(chunk * LANES, count * LANES), count * LANES)


def ratios(c_ref, h, for_model, firsts):
    hi, lo = split(h)
    model = lax.dot_general(
        for_model,
        jnp.concatenate([hi, lo, hi, lo], axis=0),
        (((0,), (0,)), ((), ())),
        preferred_element_type=F32,
    )
    counts = jnp.concatenate([c_ref[:, columns(q, NX)] for q in firsts], axis=1).astype(F32)
    r_hi, r_lo = split(counts / model)
    return jnp.concatenate([r_hi, r_lo], axis=0), jnp.concatenate([hi, lo], axis=0)


def to_row(column):
    shape = (K, LANES)
    diagonal = lax.broadcasted_iota(jnp.int32, shape, 0) == lax.broadcasted_iota(jnp.int32, shape, 1)
    return jnp.sum(jnp.where(diagonal, column, 0.0), axis=0, keepdims=True)


def to_column(row):
    shape = (K, LANES)
    diagonal = lax.broadcasted_iota(jnp.int32, shape, 0) == lax.broadcasted_iota(jnp.int32, shape, 1)
    return jnp.sum(jnp.where(diagonal, row, 0.0), axis=1, keepdims=True)


def kernel(
    c_hbm, w_hbm, h_hbm, w_out, h_out,
    c_ref, w_ref, h_in, h_ref, numer, from_core, partial, parts, row_src, row_core, row_sum, rows, y_src, y_parts,
    load_sem, core_send, core_recv, part_send, part_recv, map_send, map_recv, half_send, half_recv,
    rowc_send, rowc_recv, row_send, row_recv, y_send, y_recv,
):
    f = lax.axis_index("frames")
    y = lax.axis_index("pix")
    z, x, core = f // (2 * NX), lax.rem(f // 2, NX), lax.rem(f, 2)
    around_z = [lax.rem(z + d, NZ) for d in range(NZ)]
    around_x = [lax.rem(x + d, NX) for d in range(NX)]

    def device(dz, dx):
        return ((around_z[dz] * NX + around_x[dx]) * 2 + core, y)

    sibling = (f + 1 - 2 * core, y)
    y_devices = [(f, lax.rem(y + d, NY)) for d in Y_OFFSETS]
    own_half = core * HALF
    other_half = (1 - core) * HALF
    mine = own_half + z * NX + x

    barrier = pltpu.get_barrier_semaphore()
    for offset in OFFSETS:
        pl.semaphore_signal(barrier, inc=1, device_id=device(*offset), device_id_type=MESH)
    for d in [sibling] + y_devices:
        pl.semaphore_signal(barrier, inc=1, device_id=d, device_id_type=MESH)

    def piece_firsts(half, order, piece):
        return [half + around_z[dz] * NX for dz in order[piece * GROUPS : (piece + 1) * GROUPS]]

    load_w = pltpu.make_async_copy(w_hbm, w_ref, load_sem.at[0])
    load_h = pltpu.make_async_copy(h_hbm, h_in, load_sem.at[1])
    load_w.start()
    load_h.start()
    loads = {}
    n = 2
    for half in (1, 0):
        for piece in range(PIECES):
            loads[half, piece] = []
            for q in piece_firsts((own_half, other_half)[half], FAR_FIRST, piece):
                copy = pltpu.make_async_copy(c_hbm.at[:, columns(q, NX)], c_ref.at[:, columns(q, NX)], load_sem.at[n])
                copy.start()
                loads[half, piece].append(copy)
                n += 1

    def remote(src, dst, send, recv, to):
        return pltpu.make_async_remote_copy(
            src_ref=src, dst_ref=dst, send_sem=send, recv_sem=recv, device_id=to, device_id_type=MESH
        )

    load_w.wait()
    load_h.wait()
    w = w_ref[...]
    for it in range(ITERS):
        h_next = h_ref.at[it]

        def maps_at(q, count):
            if it == 0:
                return h_in[:, columns(q, count)]
            return jnp.concatenate([h_ref[it - 1, q + i] for i in range(count)], axis=1)

        for_model, for_maps = weight_operands(w)
        row_src[it] = to_row(jnp.sum(w, axis=1, keepdims=True))

        def numerators(half, piece, out):
            firsts = piece_firsts((own_half, other_half)[half], FAR_FIRST, piece)
            if it == 0:
                for copy in loads[half, piece]:
                    copy.wait()
            h = jnp.concatenate([maps_at(q, NX) for q in firsts], axis=1)
            rc, _ = ratios(c_ref, h, for_model, firsts)
            both = jnp.dot(for_maps, rc, preferred_element_type=F32)
            both = both[:K] + both[K:]
            for i in range(PIECE):
                out[piece * PIECE + i] = both[:, i * LANES : (i + 1) * LANES]

        def send_parts(here, part):
            band = pl.ds(part * ROWS, ROWS)
            for dz, dx in OFFSETS:
                if dz in here:
                    remote(
                        partial.at[it, FAR_FIRST.index(dz) * NX + around_x[dx], band],
                        parts.at[it, part, SLOT[dz, dx]],
                        part_send.at[it], part_recv.at[it, part], device(dz, dx),
                    ).start()

        row_copy = remote(row_src.at[it], row_core.at[it], rowc_send.at[it], rowc_recv.at[it], sibling)
        if it:
            row_copy.start()
        core_copies = []
        for piece in range(PIECES):
            numerators(1, piece, numer.at[it])
            if it == 0 and piece == 0:
                pl.semaphore_wait(barrier, len(OFFSETS) + 1 + len(y_devices))
                row_copy.start()
            chunks = pl.ds(piece * PIECE, PIECE)
            copy = remote(
                numer.at[it, chunks], from_core.at[it, chunks],
                core_send.at[it, piece], core_recv.at[it, piece], sibling,
            )
            copy.start()
            core_copies.append(copy)
        for piece in range(PIECES):
            numerators(0, piece, partial.at[it])
            if piece == 0:
                row_copy.wait()
                row_sum[it] = row_src[it] + row_core[it]
                for offset in OFFSETS:
                    remote(
                        row_sum.at[it], rows.at[it, SLOT[offset]], row_send.at[it], row_recv.at[it], device(*offset)
                    ).start()
            core_copies[piece].wait()
            chunks = pl.ds(piece * PIECE, PIECE)
            partial[it, chunks] = partial[it, chunks] + from_core[it, chunks]
            send_parts(FAR_FIRST[piece * GROUPS : (piece + 1) * GROUPS], 0)
        for part in range(1, PARTS):
            send_parts(FAR_FIRST, part)

        pltpu.make_async_copy(rows.at[it], rows.at[it], row_recv.at[it]).wait()
        c_total = to_column(row_sum[it] + jnp.sum(rows[it], axis=0))
        scale = maps_at(mine, 1) / c_total
        for part in range(PARTS):
            band = pl.ds(part * ROWS, ROWS)
            landed = parts.at[it, part]
            pltpu.make_async_copy(landed, landed, part_recv.at[it, part]).wait()
            numer_total = partial[it, FAR_FIRST.index(0) * NX + x, band] + jnp.sum(parts[it, part], axis=0)
            h_next[mine, band] = scale[part * ROWS : (part + 1) * ROWS] * numer_total
            chunk = h_next.at[mine, band]
            for dz, dx in OFFSETS:
                remote(chunk, chunk, map_send.at[it], map_recv.at[it, (NZ - dz) % NZ], device(dz, dx)).start()

        total, sums = jnp.zeros((2 * K, 2 * FRAMES), F32), jnp.zeros((K, LANES), F32)

        def weight_numerators(half, piece, total, sums):
            firsts = piece_firsts((own_half, other_half)[half], NEAR_FIRST, piece)
            h = jnp.concatenate([h_next[q + i] for q in firsts for i in range(NX)], axis=1)
            rc, hc = ratios(c_ref, h, for_model, firsts)
            total += lax.dot_general(hc, rc, (((1,), (1,)), ((), ())), preferred_element_type=F32)
            for i in range(PIECE):
                sums += h[:, i * LANES : (i + 1) * LANES]
            return total, sums

        half_copies = []
        for piece in range(PIECES):
            for dz in NEAR_FIRST[piece * GROUPS : (piece + 1) * GROUPS]:
                group = h_next.at[pl.ds(own_half + around_z[dz] * NX, NX)]
                landed = group if dz else parts.at[it, :, pl.ds(0, NX - 1)]
                pltpu.make_async_copy(landed, landed, map_recv.at[it, dz]).wait()
                copy = remote(group, group, half_send.at[it, dz], half_recv.at[it, dz], sibling)
                copy.start()
                half_copies.append(copy)
            total, sums = weight_numerators(0, piece, total, sums)
        for piece in range(PIECES):
            for copy in half_copies[piece * GROUPS : (piece + 1) * GROUPS]:
                copy.wait_recv()
            total, sums = weight_numerators(1, piece, total, sums)
        total = total[:K] + total[K:]
        total = total[:, :FRAMES] + total[:, FRAMES:]
        h_total = jnp.sum(sums, axis=1, keepdims=True)
        y_src[it] = jnp.concatenate([total, jnp.broadcast_to(h_total, (K, LANES - FRAMES))], axis=1)
        for i, to in enumerate(y_devices):
            remote(y_src.at[it], y_parts.at[it, i], y_send.at[it], y_recv.at[it], to).start()
        if it == ITERS - 1:
            for i in range(2 * HALF):
                h_in[:, i * LANES : (i + 1) * LANES] = h_next[i]
            store_h = pltpu.make_async_copy(h_in, h_out, load_sem.at[0])
            store_h.start()
        pltpu.make_async_copy(rows.at[it], rows.at[it], row_send.at[it]).wait()
        pltpu.make_async_copy(parts.at[it], parts.at[it], part_send.at[it]).wait()
        pltpu.make_async_copy(parts.at[it], parts.at[it], map_send.at[it]).wait()
        for copy in half_copies:
            copy.wait_send()
        pltpu.make_async_copy(y_parts.at[it], y_parts.at[it], y_recv.at[it]).wait()
        total = y_src[it] + jnp.sum(y_parts[it], axis=0)
        w = w * total[:, :FRAMES] / total[:, FRAMES : FRAMES + 1]
        pltpu.make_async_copy(y_parts.at[it], y_parts.at[it], y_send.at[it]).wait()
    w_out[...] = w
    store_h.wait()


def local(counts, weights, maps):
    n = len(OFFSETS)
    dma = pltpu.SemaphoreType.DMA
    anywhere = pl.BlockSpec(memory_space=pl.ANY)
    w_new, h_new = pl.pallas_call(
        kernel,
        out_shape=(jax.ShapeDtypeStruct(weights.shape, F32), jax.ShapeDtypeStruct(maps.shape, F32)),
        in_specs=[anywhere] * 3,
        out_specs=(pl.BlockSpec(memory_space=pltpu.VMEM), anywhere),
        scratch_shapes=[
            pltpu.VMEM((FRAMES, PIX), jnp.int32),
            pltpu.VMEM((K, FRAMES), F32),
            pltpu.VMEM((K, PIX), F32),
            pltpu.VMEM((ITERS, 2 * HALF, K, LANES), F32),
            pltpu.VMEM((ITERS, HALF, K, LANES), F32),
            pltpu.VMEM((ITERS, HALF, K, LANES), F32),
            pltpu.VMEM((ITERS, HALF, K, LANES), F32),
            pltpu.VMEM((ITERS, PARTS, n, ROWS, LANES), F32),
            pltpu.VMEM((ITERS, 1, LANES), F32),
            pltpu.VMEM((ITERS, 1, LANES), F32),
            pltpu.VMEM((ITERS, 1, LANES), F32),
            pltpu.VMEM((ITERS, n, 1, LANES), F32),
            pltpu.VMEM((ITERS, K, LANES), F32),
            pltpu.VMEM((ITERS, NY - 1, K, LANES), F32),
            dma((2 + 2 * NZ,)),
            dma((ITERS, PIECES)),
            dma((ITERS, PIECES)),
            dma((ITERS,)),
            dma((ITERS, PARTS)),
            dma((ITERS,)),
            dma((ITERS, NZ)),
            dma((ITERS, NZ)),
            dma((ITERS, NZ)),
            dma((ITERS,)),
            dma((ITERS,)),
            dma((ITERS,)),
            dma((ITERS,)),
            dma((ITERS,)),
            dma((ITERS,)),
        ],
        compiler_params=pltpu.CompilerParams(
            collective_id=0, has_side_effects=True, vmem_limit_bytes=53 * 1024 * 1024
        ),
        name="nmf_updates",
    )(counts, weights, maps)
    return pl.pallas_call(
        store,
        out_shape=(jax.ShapeDtypeStruct(weights.shape, F32), jax.ShapeDtypeStruct(maps.shape, F32)),
        in_specs=[pl.BlockSpec(memory_space=pltpu.VMEM)] * 2,
        out_specs=(anywhere, anywhere),
        scratch_shapes=[dma((2,))],
        compiler_params=pltpu.CompilerParams(vmem_limit_bytes=4 * 1024 * 1024),
        name="store_outputs",
    )(w_new, h_new)


def store(w_in, h_in, w_out, h_out, sems):
    copies = [pltpu.make_async_copy(w_in, w_out, sems.at[0]), pltpu.make_async_copy(h_in, h_out, sems.at[1])]
    for copy in copies:
        copy.start()
    for copy in copies:
        copy.wait()


def solution(mesh):
    return jax.shard_map(
        local,
        mesh=mesh,
        in_specs=(P("frames", "pix"), P(None, "frames"), P(None, "pix")),
        out_specs=(P(None, "frames"), P(None, "pix")),
        check_vma=False,
    )
```

time: 73.8 us -> 66.4 us (0.90)
  local copies, waits for them, and re-layouts: 4.72 us -> 0.69 us
  Pallas kernels: 68.2 us -> 64.9 us
    pallas_call x1, Pallas kernels: 68.2 us -> 64.1 us  [local(): pl.pallas_call(kernel, out_shape=(jax.ShapeDtypeStruct(weights.shape, F32...]
    unnamed x8 -> x2, local copies, waits for them, and re-layouts: 4.72 us -> 0.69 us
    pallas_call x0 -> x1, Pallas kernels: none -> 0.82 us  [local(): pl.pallas_call(store, out_shape=(jax.ShapeDtypeStruct(weights.shape, F32)...]
where the time goes in v2:
time: 66.4 us; the launch traced here: 66.3 us
  Pallas kernels  64.9 us (98%)
  local copies, waits for them, and re-layouts  0.69 us (1%)
    pallas_call x1, Pallas kernels, local(): pl.pallas_call(kernel, out_shape=(jax.ShapeDtypeStruct(weights.shape, F32...  64.1 us

profile of v2, /device:TPU:1, one launch (start us, length us, event | category | flops | bytes accessed | tf_op | source)
XLA Modules:
  0.0 66.3 jit_solution(3946107683466937612)
XLA Ops:
  0.6 0.0 copy-start
  0.6 0.7 %copy-done = f32[16,64]{1,0:T(8,128)S(1)} copy-done((f32[16,64]{1,0:T(8,128)S(1)}, f32[16,64]{1,0:T(8,128)}, u32[]{:S(2)}) %copy-start) | copy-done | bytes 4120
  1.3 64.1 %nmf_updates.1 = (f32[16,64]{1,0:T(8,128)S(1)}, f32[16,8192]{1,0:T(8,128)S(1)}) custom-call(s32[64,8192]{1,0:T(8,128)} %c_hbm.1, f32[16,64]{1,0:T(8,128)S(1)} %copy-done, f32[16,8192]{1,0:T(8,128)} %h_hbm.1), custom_call_target="tpu_custom_call" | custom-call | tf_op jit(solution)/shard_map/nmf_updates/pallas_call | solution.py:265
  65.4 0.8 %store_outputs.1 = (f32[16,64]{1,0:T(8,128)}, f32[16,8192]{1,0:T(8,128)}) custom-call(f32[16,64]{1,0:T(8,128)S(1)} %get-tuple-element.4.w_in, f32[16,8192]{1,0:T(8,128)S(1)} %get-tuple-element.5.h_in), custom_call_target="tpu_custom_call" | custom-call | tf_op jit(solution)/shard_map/store_outputs/pallas_call | solution.py:306
Async XLA Ops:
  0.6 0.7 %copy-start = (f32[16,64]{1,0:T(8,128)S(1)}, f32[16,64]{1,0:T(8,128)}, u32[]{:S(2)}) copy-start(f32[16,64]{1,0:T(8,128)} %w_hbm.1) | copy-start | bytes 12292

commit v3 on v2

--- a/solution.py
+++ b/solution.py
@@ -34,7 +34,13 @@
 GROUP_PIX = NX * LANES
 PIECE = GROUPS * NX
 PARTS = 2
+VIA_X = (4, 3, 5, 2, 6, 1, 7)
+VIA_Z = (4, 3, 5, 2, 6, 1, 7)
 ROWS = K // PARTS
+LAST = PARTS - 1
+STAGED = max(1, len(VIA_X))
+X_OFFSETS = (2, 1, 3)
+PART_OFFSETS = [[o for o in OFFSETS if part < LAST or o[0] not in VIA_X] for part in range(PARTS)]
 
 
 def split(x):
@@ -81,6 +87,7 @@
 def kernel(
     c_hbm, w_hbm, h_hbm, w_out, h_out,
     c_ref, w_ref, h_in, h_ref, numer, from_core, partial, parts, row_src, row_core, row_sum, rows, y_src, y_parts,
+    along_x, x_sum, along_z, along_x_send, along_x_recv, along_z_send, along_z_recv, first_send, first_recv,
     load_sem, core_send, core_recv, part_send, part_recv, map_send, map_recv, half_send, half_recv,
     rowc_send, rowc_recv, row_send, row_recv, y_send, y_recv,
 ):
@@ -96,6 +103,7 @@
     sibling = (f + 1 - 2 * core, y)
     y_devices = [(f, lax.rem(y + d, NY)) for d in Y_OFFSETS]
     own_half = core * HALF
+    last_band = pl.ds(LAST * ROWS, ROWS)
     other_half = (1 - core) * HALF
     mine = own_half + z * NX + x
 
@@ -156,12 +164,12 @@
 
         def send_parts(here, part):
             band = pl.ds(part * ROWS, ROWS)
-            for dz, dx in OFFSETS:
+            for slot, (dz, dx) in enumerate(PART_OFFSETS[part]):
                 if dz in here:
                     remote(
                         partial.at[it, FAR_FIRST.index(dz) * NX + around_x[dx], band],
-                        parts.at[it, part, SLOT[dz, dx]],
-                        part_send.at[it], part_recv.at[it, part], device(dz, dx),
+                        parts.at[it, part, slot],
+                        part_send.at[it, part], part_recv.at[it, part], device(dz, dx),
                     ).start()
 
         row_copy = remote(row_src.at[it], row_core.at[it], rowc_send.at[it], rowc_recv.at[it], sibling)
@@ -192,22 +200,48 @@
             core_copies[piece].wait()
             chunks = pl.ds(piece * PIECE, PIECE)
             partial[it, chunks] = partial[it, chunks] + from_core[it, chunks]
-            send_parts(FAR_FIRST[piece * GROUPS : (piece + 1) * GROUPS], 0)
+            here = FAR_FIRST[piece * GROUPS : (piece + 1) * GROUPS]
+            for i, dz in enumerate(VIA_X):
+                if dz in here:
+                    for j, dx in enumerate(X_OFFSETS):
+                        remote(
+                            partial.at[it, FAR_FIRST.index(dz) * NX + around_x[dx], last_band], along_x.at[it, i, j],
+                            along_x_send.at[it], along_x_recv.at[it, i], device(0, dx),
+                        ).start()
+            send_parts(here, 0)
         for part in range(1, PARTS):
             send_parts(FAR_FIRST, part)
+        for i, dz in enumerate(VIA_X):
+            landed = along_x.at[it, i]
+            pltpu.make_async_copy(landed, landed, along_x_recv.at[it, i]).wait()
+            x_sum[it, i] = partial[it, FAR_FIRST.index(dz) * NX + x, last_band] + jnp.sum(along_x[it, i], axis=0)
+            remote(x_sum.at[it, i], along_z.at[it, i], along_z_send.at[it], along_z_recv.at[it], device(dz, 0)).start()
 
         pltpu.make_async_copy(rows.at[it], rows.at[it], row_recv.at[it]).wait()
         c_total = to_column(row_sum[it] + jnp.sum(rows[it], axis=0))
         scale = maps_at(mine, 1) / c_total
         for part in range(PARTS):
             band = pl.ds(part * ROWS, ROWS)
-            landed = parts.at[it, part]
+            count = len(PART_OFFSETS[part])
+            landed = parts.at[it, part, pl.ds(0, count)]
             pltpu.make_async_copy(landed, landed, part_recv.at[it, part]).wait()
-            numer_total = partial[it, FAR_FIRST.index(0) * NX + x, band] + jnp.sum(parts[it, part], axis=0)
+            numer_total = partial[it, FAR_FIRST.index(0) * NX + x, band] + jnp.sum(parts[it, part, :count], axis=0)
+            if VIA_X and part == LAST:
+                pltpu.make_async_copy(along_z.at[it], along_z.at[it], along_z_recv.at[it]).wait()
+                numer_total += jnp.sum(along_z[it], axis=0)
             h_next[mine, band] = scale[part * ROWS : (part + 1) * ROWS] * numer_total
             chunk = h_next.at[mine, band]
+            if part == 0:
+                for dz in VIA_Z:
+                    remote(chunk, chunk, first_send.at[it], first_recv.at[it, (NZ - dz) % NZ], device(dz, 0)).start()
             for dz, dx in OFFSETS:
-                remote(chunk, chunk, map_send.at[it], map_recv.at[it, (NZ - dz) % NZ], device(dz, dx)).start()
+                if part or dz not in VIA_Z:
+                    remote(chunk, chunk, map_send.at[it], map_recv.at[it, (NZ - dz) % NZ], device(dz, dx)).start()
+        for dz in VIA_Z[::-1]:
+            chunk = h_next.at[own_half + around_z[dz] * NX + x, pl.ds(0, ROWS)]
+            pltpu.make_async_copy(chunk, chunk, first_recv.at[it, dz]).wait()
+            for dx in X_OFFSETS:
+                remote(chunk, chunk, first_send.at[it], map_recv.at[it, dz], device(0, dx)).start()
 
         total, sums = jnp.zeros((2 * K, 2 * FRAMES), F32), jnp.zeros((K, LANES), F32)
 
@@ -224,7 +258,8 @@
         for piece in range(PIECES):
             for dz in NEAR_FIRST[piece * GROUPS : (piece + 1) * GROUPS]:
                 group = h_next.at[pl.ds(own_half + around_z[dz] * NX, NX)]
-                landed = group if dz else parts.at[it, :, pl.ds(0, NX - 1)]
+                bands = 6 if dz == 0 else 7 if dz in VIA_Z else 8
+                landed = parts.at[it, 0, pl.ds(0, bands)]
                 pltpu.make_async_copy(landed, landed, map_recv.at[it, dz]).wait()
                 copy = remote(group, group, half_send.at[it, dz], half_recv.at[it, dz], sibling)
                 copy.start()
@@ -246,8 +281,17 @@
             store_h = pltpu.make_async_copy(h_in, h_out, load_sem.at[0])
             store_h.start()
         pltpu.make_async_copy(rows.at[it], rows.at[it], row_send.at[it]).wait()
-        pltpu.make_async_copy(parts.at[it], parts.at[it], part_send.at[it]).wait()
-        pltpu.make_async_copy(parts.at[it], parts.at[it], map_send.at[it]).wait()
+        for part in range(PARTS):
+            landed = parts.at[it, part, pl.ds(0, len(PART_OFFSETS[part]))]
+            pltpu.make_async_copy(landed, landed, part_send.at[it, part]).wait()
+        if VIA_X:
+            pltpu.make_async_copy(along_x.at[it], along_x.at[it], along_x_send.at[it]).wait()
+            pltpu.make_async_copy(along_z.at[it], along_z.at[it], along_z_send.at[it]).wait()
+        landed = h_next.at[pl.ds(0, len(OFFSETS) - 2 * len(VIA_Z))]
+        pltpu.make_async_copy(landed, landed, map_send.at[it]).wait()
+        if VIA_Z:
+            landed = h_next.at[pl.ds(0, 2 * len(VIA_Z))]
+            pltpu.make_async_copy(landed, landed, first_send.at[it]).wait()
         for copy in half_copies:
             copy.wait_send()
         pltpu.make_async_copy(y_parts.at[it], y_parts.at[it], y_recv.at[it]).wait()
@@ -282,10 +326,19 @@
             pltpu.VMEM((ITERS, n, 1, LANES), F32),
             pltpu.VMEM((ITERS, K, LANES), F32),
             pltpu.VMEM((ITERS, NY - 1, K, LANES), F32),
+            pltpu.VMEM((ITERS, STAGED, NX - 1, ROWS, LANES), F32),
+            pltpu.VMEM((ITERS, STAGED, ROWS, LANES), F32),
+            pltpu.VMEM((ITERS, STAGED, ROWS, LANES), F32),
+            dma((ITERS,)),
+            dma((ITERS, STAGED)),
+            dma((ITERS,)),
+            dma((ITERS,)),
+            dma((ITERS,)),
+            dma((ITERS, NZ)),
             dma((2 + 2 * NZ,)),
             dma((ITERS, PIECES)),
             dma((ITERS, PIECES)),
-            dma((ITERS,)),
+            dma((ITERS, PARTS)),
             dma((ITERS, PARTS)),
             dma((ITERS,)),
             dma((ITERS, NZ)),

time: 66.4 us -> 64.3 us (0.968)
  Pallas kernels: 64.9 us -> 62.8 us
    pallas_call x1, Pallas kernels: 64.1 us -> 62 us  [local(): pl.pallas_call(kernel, out_shape=(jax.ShapeDtypeStruct(weights.shape, F32...]
where the time goes in v3:
time: 64.3 us; the launch traced here: 64.2 us
  Pallas kernels  62.8 us (98%)
  local copies, waits for them, and re-layouts  0.69 us (1%)
  between operations  0.65 us (1%)
    pallas_call x1, Pallas kernels, local(): pl.pallas_call(kernel, out_shape=(jax.ShapeDtypeStruct(weights.shape, F32...  62 us

profile of v3, /device:TPU:1, one launch (start us, length us, event | category | flops | bytes accessed | tf_op | source)
XLA Modules:
  0.0 64.2 jit_solution(3493798743677569664)
XLA Ops:
  0.6 0.0 copy-start
  0.6 0.7 %copy-done = f32[16,64]{1,0:T(8,128)S(1)} copy-done((f32[16,64]{1,0:T(8,128)S(1)}, f32[16,64]{1,0:T(8,128)}, u32[]{:S(2)}) %copy-start) | copy-done | bytes 4120
  1.3 62.0 %nmf_updates.1 = (f32[16,64]{1,0:T(8,128)S(1)}, f32[16,8192]{1,0:T(8,128)S(1)}) custom-call(s32[64,8192]{1,0:T(8,128)} %c_hbm.1, f32[16,64]{1,0:T(8,128)S(1)} %copy-done, f32[16,8192]{1,0:T(8,128)} %h_hbm.1), custom_call_target="tpu_custom_call" | custom-call | tf_op jit(solution)/shard_map/nmf_updates/pallas_call | solution.py:309
  63.3 0.8 %store_outputs.1 = (f32[16,64]{1,0:T(8,128)}, f32[16,8192]{1,0:T(8,128)}) custom-call(f32[16,64]{1,0:T(8,128)S(1)} %get-tuple-element.4.w_in, f32[16,8192]{1,0:T(8,128)S(1)} %get-tuple-element.5.h_in), custom_call_target="tpu_custom_call" | custom-call | tf_op jit(solution)/shard_map/store_outputs/pallas_call | solution.py:359
Async XLA Ops:
  0.6 0.7 %copy-start = (f32[16,64]{1,0:T(8,128)S(1)}, f32[16,64]{1,0:T(8,128)}, u32[]{:S(2)}) copy-start(f32[16,64]{1,0:T(8,128)} %w_hbm.1) | copy-start | bytes 12292

commit v4 on v3

--- a/solution.py
+++ b/solution.py
@@ -28,7 +28,8 @@
 SLOT = {offset: i for i, offset in enumerate(OFFSETS)}
 Y_OFFSETS = (4, 3, 5, 2, 6, 1, 7)
 FAR_FIRST = (4, 3, 5, 2, 6, 1, 7, 0)
-NEAR_FIRST = (0, 1, 7, 2, 6, 3, 5, 4)
+GATHERED = ((0, 1, 7), (2, 6, 3), (5, 4))
+ORDER = (('forward', 0), ('own', 0), ('forward', 1), ('forward', 2), ('own', 1), ('sibling', 0), ('own', 2), ('sibling', 1), ('sibling', 2))
 GROUPS = 4
 PIECES = NZ // GROUPS
 GROUP_PIX = NX * LANES
@@ -40,7 +41,7 @@
 LAST = PARTS - 1
 STAGED = max(1, len(VIA_X))
 X_OFFSETS = (2, 1, 3)
-PART_OFFSETS = [[o for o in OFFSETS if part < LAST or o[0] not in VIA_X] for part in range(PARTS)]
+PART_OFFSETS = [[o for o in sorted(OFFSETS, key=lambda o: -hops(o)) if part < LAST or o[0] not in VIA_X] for part in range(PARTS)]
 
 
 def split(x):
@@ -245,30 +246,32 @@
 
         total, sums = jnp.zeros((2 * K, 2 * FRAMES), F32), jnp.zeros((K, LANES), F32)
 
-        def weight_numerators(half, piece, total, sums):
-            firsts = piece_firsts((own_half, other_half)[half], NEAR_FIRST, piece)
+        def weight_numerators(half, groups, total, sums):
+            firsts = [(own_half, other_half)[half] + around_z[dz] * NX for dz in groups]
             h = jnp.concatenate([h_next[q + i] for q in firsts for i in range(NX)], axis=1)
             rc, hc = ratios(c_ref, h, for_model, firsts)
             total += lax.dot_general(hc, rc, (((1,), (1,)), ((), ())), preferred_element_type=F32)
-            for i in range(PIECE):
+            for i in range(len(groups) * NX):
                 sums += h[:, i * LANES : (i + 1) * LANES]
             return total, sums
 
-        half_copies = []
-        for piece in range(PIECES):
-            for dz in NEAR_FIRST[piece * GROUPS : (piece + 1) * GROUPS]:
-                group = h_next.at[pl.ds(own_half + around_z[dz] * NX, NX)]
-                bands = 6 if dz == 0 else 7 if dz in VIA_Z else 8
-                landed = parts.at[it, 0, pl.ds(0, bands)]
-                pltpu.make_async_copy(landed, landed, map_recv.at[it, dz]).wait()
-                copy = remote(group, group, half_send.at[it, dz], half_recv.at[it, dz], sibling)
-                copy.start()
-                half_copies.append(copy)
-            total, sums = weight_numerators(0, piece, total, sums)
-        for piece in range(PIECES):
-            for copy in half_copies[piece * GROUPS : (piece + 1) * GROUPS]:
-                copy.wait_recv()
-            total, sums = weight_numerators(1, piece, total, sums)
+        half_copies = {}
+        for step, piece in ORDER:
+            groups = GATHERED[piece]
+            if step == "forward":
+                for dz in groups:
+                    group = h_next.at[pl.ds(own_half + around_z[dz] * NX, NX)]
+                    bands = 6 if dz == 0 else 7 if dz in VIA_Z else 8
+                    landed = parts.at[it, 0, pl.ds(0, bands)]
+                    pltpu.make_async_copy(landed, landed, map_recv.at[it, dz]).wait()
+                    half_copies[dz] = remote(group, group, half_send.at[it, dz], half_recv.at[it, dz], sibling)
+                    half_copies[dz].start()
+            elif step == "own":
+                total, sums = weight_numerators(0, groups, total, sums)
+            else:
+                for dz in groups:
+                    half_copies[dz].wait_recv()
+                total, sums = weight_numerators(1, groups, total, sums)
         total = total[:K] + total[K:]
         total = total[:, :FRAMES] + total[:, FRAMES:]
         h_total = jnp.sum(sums, axis=1, keepdims=True)
@@ -292,7 +295,7 @@
         if VIA_Z:
             landed = h_next.at[pl.ds(0, 2 * len(VIA_Z))]
             pltpu.make_async_copy(landed, landed, first_send.at[it]).wait()
-        for copy in half_copies:
+        for copy in half_copies.values():
             copy.wait_send()
         pltpu.make_async_copy(y_parts.at[it], y_parts.at[it], y_recv.at[it]).wait()
         total = y_src[it] + jnp.sum(y_parts[it], axis=0)

time: 64.3 us -> 64.3 us (level)
  no operation moved by 1% of the time
where the time goes in v4:
time: 64.3 us; the launch traced here: 64.1 us
  Pallas kernels  62.7 us (98%)
  local copies, waits for them, and re-layouts  0.69 us (1%)
  between operations  0.65 us (1%)
    pallas_call x1, Pallas kernels, local(): pl.pallas_call(kernel, out_shape=(jax.ShapeDtypeStruct(weights.shape, F32...  61.9 us

profile of v4, /device:TPU:1, one launch (start us, length us, event | category | flops | bytes accessed | tf_op | source)
XLA Modules:
  0.0 64.1 jit_solution(61122304573713095)
XLA Ops:
  0.6 0.0 copy-start
  0.6 0.7 %copy-done = f32[16,64]{1,0:T(8,128)S(1)} copy-done((f32[16,64]{1,0:T(8,128)S(1)}, f32[16,64]{1,0:T(8,128)}, u32[]{:S(2)}) %copy-start) | copy-done | bytes 4120
  1.3 61.9 %nmf_updates.1 = (f32[16,64]{1,0:T(8,128)S(1)}, f32[16,8192]{1,0:T(8,128)S(1)}) custom-call(s32[64,8192]{1,0:T(8,128)} %c_hbm.1, f32[16,64]{1,0:T(8,128)S(1)} %copy-done, f32[16,8192]{1,0:T(8,128)} %h_hbm.1), custom_call_target="tpu_custom_call" | custom-call | tf_op jit(solution)/shard_map/nmf_updates/pallas_call | solution.py:312
  63.3 0.8 %store_outputs.1 = (f32[16,64]{1,0:T(8,128)}, f32[16,8192]{1,0:T(8,128)}) custom-call(f32[16,64]{1,0:T(8,128)S(1)} %get-tuple-element.4.w_in, f32[16,8192]{1,0:T(8,128)S(1)} %get-tuple-element.5.h_in), custom_call_target="tpu_custom_call" | custom-call | tf_op jit(solution)/shard_map/store_outputs/pallas_call | solution.py:362
Async XLA Ops:
  0.6 0.7 %copy-start = (f32[16,64]{1,0:T(8,128)S(1)}, f32[16,64]{1,0:T(8,128)}, u32[]{:S(2)}) copy-start(f32[16,64]{1,0:T(8,128)} %w_hbm.1) | copy-start | bytes 12292
